TPU v7x, 256 devices: a whole 4x4x8 slice. The times are simulated.
256 devices in a mesh: ctx: 32 (over x_lo, z, core), dp: 8 (over y, x_hi).
Axes of the slice: x: 4 (x_hi: 2, x_lo: 2; x = x_hi * 2 + x_lo), y: 4, z: 8, core: 2. Of those that a mesh axis runs over, the one named last changes fastest.
Arguments:
- q_nope: bfloat16 [8, 4096, 2048], P('dp', 'ctx'), may hold values from -8 to 8
- q_rope: bfloat16 [8, 4096, 1024], P('dp', 'ctx'), may hold values from -8 to 8
- dout: bfloat16 [8, 4096, 2048], P('dp', 'ctx'), may hold values from -8 to 8
- latent: bfloat16 [8, 4096, 512], P('dp', 'ctx'), may hold values from -8 to 8
- rope_key: bfloat16 [8, 4096, 64], P('dp', 'ctx'), may hold values from -8 to 8
- doc_ids: int32 [8, 4096], P('dp'), may hold values from 0 to 16, as said below
- w_up: bfloat16 [4096, 512], replicated, may hold values from -0.25 to 0.25
Outputs:
- q_nope_grad: bfloat16 [8, 4096, 2048], P('dp', 'ctx')
- q_rope_grad: bfloat16 [8, 4096, 1024], P('dp', 'ctx')
- latent_grad: float32 [8, 4096, 512], P('dp', 'ctx')
- rope_key_grad: float32 [8, 4096, 64], P('dp', 'ctx')
- up_grad: float32 [4096, 512], P(('ctx', 'dp'))
Inputs may be any that keep to these rules, and one draw needn't show every extreme that they name: `doc_ids`: numbers start at 0 at each sequence's first token; each token's number equals its predecessor's or exceeds it by one; every sequence's last number is 16.
All inputs are finite; a program needn't handle non-finite values.
Results may differ from a plain program's by a relative error of at most 0.012.
Values may be sent and summed in bfloat16 or wider, within the bound.
A program may use at most 64 MiB of HBM per device.

v0:
```python
import jax
import jax.numpy as jnp
from jax import lax
from jax.sharding import PartitionSpec as P

ROPE = 64
HEAD_DIM = 128
HEADS = 16
BAND = 2


def from_behind(value, axis, steps):
    count = lax.axis_size(axis)
    first, last = (max(0, -steps), min(count, count - steps))
    return lax.ppermute(value, axis, [(source, source + steps) for source in range(first, last)])


def shortened(value):
    return jax.tree.map(lambda a: a.astype(jnp.bfloat16) if a.dtype == jnp.float32 else a, value)


def expand(latent_rows, w_up):
    return lax.dot_general(
        latent_rows, w_up, (((1,), (1,)), ((), ())), preferred_element_type=jnp.float32
    ).astype(jnp.bfloat16)


def split_pair(values):
    high_part = lax.optimization_barrier(values.astype(jnp.bfloat16))
    low_part = (values - high_part.astype(jnp.float32)).astype(jnp.bfloat16)
    return (high_part, low_part)


def project_pair(grad_values, w_up):
    high_part, low_part = split_pair(grad_values)
    row_count = grad_values.shape[0]
    stacked = jnp.concatenate([high_part, low_part], axis=0)
    both = jnp.dot(stacked, w_up, preferred_element_type=jnp.float32)
    return both[:row_count] + both[row_count:]


def visible_mask(doc_row, block_index, block_rows):
    lead_rows = BAND * block_rows
    query_pos = block_index * block_rows + jnp.arange(block_rows, dtype=jnp.int32)
    key_pos = (
        block_index * block_rows - lead_rows + jnp.arange(lead_rows + block_rows, dtype=jnp.int32)
    )
    doc_pad = jnp.concatenate([jnp.full((lead_rows,), -1, jnp.int32), doc_row], axis=0)
    query_docs = lax.dynamic_slice_in_dim(doc_row, block_index * block_rows, block_rows)
    key_docs = lax.dynamic_slice_in_dim(doc_pad, block_index * block_rows, lead_rows + block_rows)
    return (
        (key_pos[None, :] <= query_pos[:, None])
        & (query_pos[:, None] - key_pos[None, :] < lead_rows)
        & (query_docs[:, None] == key_docs[None, :])
    )


def attend(query_nope, query_rope, grads_out, keys_values, rope_keys, visible):
    rows_query = query_nope.shape[0]
    rows_key = keys_values.shape[0]
    scale_factor = float(HEAD_DIM + ROPE) ** (-0.5)
    split_at = HEADS * HEAD_DIM
    queries = query_nope.reshape(rows_query, HEADS, HEAD_DIM)
    rotary_q = query_rope.reshape(rows_query, HEADS, ROPE)
    grad_heads = grads_out.reshape(rows_query, HEADS, HEAD_DIM)
    keys_nope = keys_values[:, :split_at].reshape(rows_key, HEADS, HEAD_DIM)
    values_all = keys_values[:, split_at:].reshape(rows_key, HEADS, HEAD_DIM)
    wide = jnp.float32
    scores = (
        jnp.einsum("qhd,khd->hqk", queries, keys_nope, preferred_element_type=wide)
        + jnp.einsum("qhr,kr->hqk", rotary_q, rope_keys, preferred_element_type=wide)
    ) * scale_factor
    scores = jnp.where(visible[None], scores, -jnp.inf)
    highest = jnp.max(scores, axis=-1, keepdims=True)
    weights = jnp.exp(scores - highest)
    probs = weights / jnp.sum(weights, axis=-1, keepdims=True)
    probs_low = probs.astype(jnp.bfloat16)
    outputs = jnp.einsum("hqk,khd->qhd", probs_low, values_all, preferred_element_type=wide)
    delta = jnp.sum(grad_heads.astype(wide) * outputs, axis=-1)
    grad_probs = jnp.einsum("qhd,khd->hqk", grad_heads, values_all, preferred_element_type=wide)
    grad_scores = (probs * (grad_probs - delta.T[:, :, None]) * scale_factor).astype(jnp.bfloat16)
    query_grad = jnp.einsum(
        "hqk,khd->qhd", grad_scores, keys_nope, preferred_element_type=wide
    ).reshape(rows_query, -1)
    rotary_grad = jnp.einsum(
        "hqk,kr->qhr", grad_scores, rope_keys, preferred_element_type=wide
    ).reshape(rows_query, -1)
    key_grad = jnp.einsum(
        "hqk,qhd->khd", grad_scores, queries, preferred_element_type=wide
    ).reshape(rows_key, -1)
    value_grad = jnp.einsum(
        "hqk,qhd->khd", probs_low, grad_heads, preferred_element_type=wide
    ).reshape(rows_key, -1)
    rope_grad = jnp.einsum("hqk,qhr->kr", grad_scores, rotary_q, preferred_element_type=wide)
    return (query_grad, rotary_grad, jnp.concatenate([key_grad, value_grad], axis=1), rope_grad)


def body(q_nope, q_rope, dout, latent, rope_key, doc_ids, w_up):
    block_rows = latent.shape[1]
    block_index = lax.axis_index("ctx")
    visible = visible_mask(doc_ids[0], block_index, block_rows)
    own_latent = latent[0]
    own_rope = rope_key[0]
    arriving = (expand(own_latent, w_up), own_rope)
    kv_seen = [arriving[0]]
    rope_seen = [arriving[1]]
    for travel in range(BAND):
        arriving = from_behind((arriving[0], arriving[1]), "ctx", 1)
        kv_seen.append(arriving[0])
        rope_seen.append(arriving[1])
    keys_values = jnp.concatenate(kv_seen[::-1], axis=0)
    rope_keys = jnp.concatenate(rope_seen[::-1], axis=0)
    query_grad, rotary_grad, key_grads, rope_grads = attend(
        q_nope[0], q_rope[0], dout[0], keys_values, rope_keys, visible
    )
    carried = (key_grads[:block_rows], rope_grads[:block_rows])
    for travel in range(BAND):
        carried = from_behind((shortened(carried[0]), shortened(carried[1])), "ctx", -1)
        lower = (travel + 1) * block_rows
        carried = (
            carried[0] + key_grads[lower : lower + block_rows],
            carried[1] + rope_grads[lower : lower + block_rows],
        )
    grad_total, rope_total = carried
    latent_grad = project_pair(grad_total, w_up)
    grad_high, grad_low = split_pair(grad_total)
    latent_twice = jnp.concatenate([own_latent, own_latent], axis=0)
    stacked = jnp.concatenate([grad_high, grad_low], axis=0)
    up_grad = lax.psum_scatter(
        lax.dot_general(
            stacked, latent_twice, (((0,), (0,)), ((), ())), preferred_element_type=jnp.float32
        ),
        ("ctx", "dp"),
        scatter_dimension=0,
        tiled=True,
    )
    return (
        query_grad.astype(jnp.bfloat16)[None],
        rotary_grad.astype(jnp.bfloat16)[None],
        latent_grad[None],
        rope_total[None],
        up_grad,
    )


def solution(mesh):
    return jax.shard_map(
        body,
        mesh=mesh,
        in_specs=(
            P("dp", "ctx", None),
            P("dp", "ctx", None),
            P("dp", "ctx", None),
            P("dp", "ctx", None),
            P("dp", "ctx", None),
            P("dp", None),
            P(),
        ),
        out_specs=(
            P("dp", "ctx", None),
            P("dp", "ctx", None),
            P("dp", "ctx", None),
            P("dp", "ctx", None),
            P(("ctx", "dp"), None),
        ),
        check_vma=False,
    )
```

profile of v0, /device:TPU:128, one launch (start us, length us, event | category | flops | bytes accessed | tf_op | source)
XLA Modules:
  0.0 1444.0 jit_solution(8546803126103041074)
XLA Ops:
  7.2 0.0 reduce-scatter.2.cloned.1.call-start
  7.2 3.7 convolution_convert_fusion
  11.0 1.9 collective-permute-start
  12.9 15.4 %collective-permute-done = bf16[128,4096]{1,0:T(8,128)(2,1)S(1)} collective-permute-done((bf16[128,4096]{1,0:T(8,128)(2,1)S(1)}, bf16[128,4096]{1,0:T(8,128)(2,1)S(1)}, u32[]{:S(2)}, u32[]{:S(2)}) %collective-permute-start) | collective-permute-done | bytes 1048608 | tf_op jit(solution)/shard_map/ppermute | solution.py:15
  28.3 1.9 collective-permute-start.1
  30.2 1.9 collective-permute-start.2
  32.2 0.1 pad_dynamic-slice_fusion
  32.3 0.2 fusion.21
  32.5 2.0 copy.33
  34.5 2.1 copy.55
  36.6 1.1 copy.32
  37.7 8.1 collective-permute-done.2
  45.8 1.9 collective-permute-start.3
  47.7 0.3 pad_maximum_fusion
  48.0 1.4 fusion.34
  49.4 1.9 copy.54
  51.3 3.7 fusion.36
  55.0 1.6 copy.56
  56.6 2.5 fusion.4
  59.1 2.6 fusion.35
  61.7 4.0 fusion.29
  65.7 4.5 fusion.15
  70.2 3.5 fusion.2
  73.7 0.8 fusion.37
  74.5 0.1 fusion.9
  74.6 0.2 copy-done
  74.9 4.8 collective-permute-start.4
  79.7 12.3 collective-permute-done.4
  92.0 0.3 fusion.7
  92.3 5.0 collective-permute-start.5
  97.3 12.3 collective-permute-done.5
  109.6 0.3 fusion.32
  109.9 0.2 subtract_convert_fusion
  110.1 0.8 copy-done.5
  110.9 0.4 copy-done.7
  111.3 4.5 fusion.12
  115.8 1.4 copy-done.1
  117.2 0.6 convolution_bitcast_fusion.1
  117.8 5.0 collective-permute-start.6
  122.8 1.4 convolution_convert_fusion.1
  124.3 4.8 collective-permute-start.7
  129.1 0.4 convolution_convert_fusion.2
  129.5 2.0 copy.45
  131.6 0.8 copy.46
  132.4 0.6 fusion.22
  133.0 4.1 fusion.13
  137.1 0.7 fusion.16
  137.9 1299.3 %reduce-scatter.2.cloned.1.call-done = f32[16,512]{1,0:T(8,128)} async-done(((f32[4096,512]{1,0:T(8,128)}), f32[16,512]{1,0:T(8,128)}) %reduce-scatter.2.cloned.1.call-update) | async-done | bytes 32784 | tf_op jit(solution)/shard_map/reduce_scatter | solution.py:129
  (27 shorter events, 0.1 us)
Async XLA Ops:
  7.2 23.1 %copy-start.9 = (bf16[1,128,64]{1,2,0:T(8,128)(2,1)S(1)}, bf16[1,128,64]{1,2,0:T(8,128)(2,1)}, u32[]{:S(2)}) copy-start(bf16[1,128,64]{1,2,0:T(8,128)(2,1)} %param.11) | copy-start | bytes 49156
  7.2 25.0 %copy-start.10 = (s32[1,4096]{1,0:T(1,128)S(1)}, s32[1,4096]{1,0:T(1,128)}, u32[]{:S(2)}) copy-start(s32[1,4096]{1,0:T(1,128)} %param.12) | copy-start | bytes 49156
  7.2 1430.0 %reduce-scatter.2.cloned.1.call-start = ((), (), s32[]{:S(2)}) async-start(), calls=%async_computation.1 | async-start | bytes 8421376 | tf_op jit(solution)/shard_map/reduce_scatter | solution.py:129
  11.0 17.3 %collective-permute-start = (bf16[128,4096]{1,0:T(8,128)(2,1)S(1)}, bf16[128,4096]{1,0:T(8,128)(2,1)S(1)}, u32[]{:S(2)}, u32[]{:S(2)}) collective-permute-start(bf16[128,4096]{1,0:T(8,128)(2,1)S(1)} %convolution_convert_fusion), channel_id=1, source_target_pairs={{0,8},{8,16},{16,24},{24,32},{32,40},{40,48},{48,56},{56,64},{64,7... | collective-permute-start | bytes 3145736 | tf_op jit(solution)/shard_map/ppermute | solution.py:15
  28.3 19.4 %collective-permute-start.1 = (bf16[128,4096]{1,0:T(8,128)(2,1)S(1)}, bf16[128,4096]{1,0:T(8,128)(2,1)S(1)}, u32[]{:S(2)}, u32[]{:S(2)}) collective-permute-start(bf16[128,4096]{1,0:T(8,128)(2,1)S(1)} %collective-permute-done), channel_id=1, source_target_pairs={{0,8},{8,16},{16,24},{24,32},{32,40},{40,48},{48,56},{56,64},{64,7... | collective-permute-start | bytes 3145736 | tf_op jit(solution)/shard_map/ppermute | solution.py:15
  30.2 15.6 %collective-permute-start.2 = (bf16[128,64]{0,1:T(8,128)(2,1)S(1)}, bf16[128,64]{0,1:T(8,128)(2,1)S(1)}, u32[]{:S(2)}, u32[]{:S(2)}) collective-permute-start(bf16[128,64]{0,1:T(8,128)(2,1)S(1)} %bitcast.94), channel_id=1, source_target_pairs={{0,8},{8,16},{16,24},{24,32},{32,40},{40,48},{48,56},{56,64},{64,7... | collective-permute-start | bytes 49160 | tf_op jit(solution)/shard_map/ppermute | solution.py:15
  45.8 10.8 collective-permute-start.3
  51.3 5.3 copy-start.2
  59.1 2.6 copy-start.4
  70.2 3.5 copy-start.6
  73.7 1.1 copy-start
  74.9 17.1 %collective-permute-start.4 = (bf16[128,4096]{0,1:T(8,128)(2,1)S(1)}, bf16[128,4096]{0,1:T(8,128)(2,1)S(1)}, u32[]{:S(2)}, u32[]{:S(2)}) collective-permute-start(bf16[128,4096]{0,1:T(8,128)(2,1)S(1)} %fusion.9), channel_id=1, source_target_pairs={{8,0},{16,8},{24,16},{32,24},{40,32},{48,40},{56,48},{64,56},{72,6... | collective-permute-start | bytes 3145736 | tf_op jit(solution)/shard_map/ppermute | solution.py:15
  92.3 17.3 %collective-permute-start.5 = (bf16[128,4096]{0,1:T(8,128)(2,1)S(1)}, bf16[128,4096]{0,1:T(8,128)(2,1)S(1)}, u32[]{:S(2)}, u32[]{:S(2)}) collective-permute-start(bf16[128,4096]{0,1:T(8,128)(2,1)S(1)} %fusion.7), channel_id=1, source_target_pairs={{8,0},{16,8},{24,16},{32,24},{40,32},{48,40},{56,48},{64,56},{72,6... | collective-permute-start | bytes 3145736 | tf_op jit(solution)/shard_map/ppermute | solution.py:15
  109.9 1.0 copy-start.5
  109.9 1.4 copy-start.8
  110.1 1.2 copy-start.7
  115.8 1.4 copy-start.1
  115.8 7.1 copy-start.3
  117.8 6.5 collective-permute-start.6
  124.3 8.1 collective-permute-start.7
Sparse Core Ops, SparseCore 0:
  115.9 1321.1 reduce-scatter.1
where the time goes:
time: 1440 us
  waiting for transfers between devices  1350 us (94%)
  matrix products  33.7 us (2%)
  starting transfers between devices  27.4 us (2%)
  local copies, waits for them, and re-layouts  15.9 us (1%)
  between operations  14.4 us (1%)
    reduce_scatter x1, waiting for transfers between devices, body(): lax.psum_scatter(lax.dot_general(stacked, latent_twice, (((0,), (0,)), ((...  1300 us
    ppermute x8, waiting for transfers between devices, from_behind(): lax.ppermute(value, axis, [(source, source + steps) for source in range(f...  48.1 us
  transfers between devices with their start and end apart: 9, of which 5 were waited for; matrix products, arithmetic and copies ran while one was open for 2% of the time, Pallas kernels for 0%

commit v1 on v0

v1 whole, which is shorter than its diff:
```python
import functools

import jax
import jax.numpy as jnp
from jax import lax
from jax.experimental import pallas as pl
from jax.experimental.pallas import tpu as pltpu
from jax.sharding import PartitionSpec as P

LATENT = 512
ROPE = 64
DIM = 128
BLOCK = 128
PAIRS = 8
CHIPS = 16
LAG = 2
STEPS = 4
SCALE = float(DIM + ROPE) ** -0.5
LOG2E = 1.4426950408889634
F32 = jnp.float32
BF16 = jnp.bfloat16


def nt(a, b):
    return lax.dot_general(a, b, (((1,), (1,)), ((), ())), preferred_element_type=F32)


def nn(a, b):
    return lax.dot_general(a, b, (((1,), (0,)), ((), ())), preferred_element_type=F32)


def tn(a, b):
    return lax.dot_general(a, b, (((0,), (0,)), ((), ())), preferred_element_type=F32)


def kernel(
    q_nope, q_rope, dout, latent, rope_key, docs, w_up,
    qn_out, qr_out, lat_out, rope_out, up_out,
    lat, ropes, rope_tile, doc_row, bias, w, qd, qg, qr_in, gkv, rope_grad, lgf, lgs, lgr,
    part, in1, out2, in2, total, out3, in3, out4, in4, zf, zb, zin,
    local_sem, head_sem, w_sem, qn_sem,
    lat_send, lat_recv, q_send, q_recv, g_send, g_recv, lg_send, lg_recv,
    rs_send, rs_recv, z_send, z_recv,
):
    ctx = lax.axis_index("ctx")
    dp = lax.axis_index("dp")
    core = lax.rem(ctx, 2)
    other = 1 - core
    chip = lax.div(ctx, 2)
    x_lo, z = lax.div(chip, PAIRS), lax.rem(chip, PAIRS)
    y, x_hi = lax.div(dp, 2), lax.rem(dp, 2)
    y_hi, y_lo = lax.div(y, 2), lax.rem(y, 2)

    def at(ctx_index, dp_index):
        return {"ctx": ctx_index, "dp": dp_index}

    def place(xh, xl, yh, yl, zz):
        return at((xl * PAIRS + zz) * 2 + core, (yh * 2 + yl) * 2 + xh)

    sibling = at(chip * 2 + other, dp)
    after = at(lax.rem(chip + 1, CHIPS) * 2 + core, dp)
    before = at(lax.rem(chip + CHIPS - 1, CHIPS) * 2 + core, dp)
    x_one = place(x_hi, 1 - x_lo, y_hi, y_lo, z)
    x_two = place(1 - x_hi, 1 - x_lo, y_hi, y_lo, z)
    y_one = place(x_hi, x_lo, y_hi, 1 - y_lo, z)
    y_two = place(x_hi, x_lo, 1 - y_hi, 1 - y_lo, z)
    x_p = (lax.rem(x_hi + x_lo, 2), x_hi, x_one, x_two)
    x_q = (x_hi, x_lo, x_two, x_one)
    y_p = (lax.rem(y_hi + y_lo, 2), y_hi, y_one, y_two)
    y_q = (y_hi, y_lo, y_two, y_one)
    first = (x_p, x_q, y_p, y_q)
    second = (y_p, y_q, x_p, x_q)

    own_rows = pl.ds(pl.multiple_of(core * BLOCK, BLOCK), BLOCK)
    sib_rows = pl.ds(pl.multiple_of(other * BLOCK, BLOCK), BLOCK)

    def lat_rows(slot):
        return pl.ds(pl.multiple_of(slot * BLOCK, BLOCK), BLOCK)

    def columns(index):
        return pl.ds(pl.multiple_of(index * DIM, DIM), DIM)

    def remote(src, dst, send, recv, device):
        return pltpu.make_async_remote_copy(
            src_ref=src, dst_ref=dst, send_sem=send, recv_sem=recv,
            device_id=device, device_id_type=pl.DeviceIdType.MESH,
        )

    pltpu.make_async_copy(latent, lat.at[lat_rows(2 + core)], local_sem.at[0]).start()
    pltpu.make_async_copy(rope_key, ropes.at[2 + core], local_sem.at[1]).start()
    behind = lax.rem(chip + CHIPS - 1, CHIPS)
    doc_copies = (
        pltpu.make_async_copy(
            docs.at[:, pl.ds(pl.multiple_of(behind * 256, 256), 256)],
            doc_row.at[:, pl.ds(0, 256)], local_sem.at[2]),
        pltpu.make_async_copy(
            docs.at[:, pl.ds(pl.multiple_of(chip * 256, 256), 256)],
            doc_row.at[:, pl.ds(256, 256)], local_sem.at[3]),
    )
    for copy in doc_copies:
        copy.start()

    def load_head(j, _):
        head = 2 * j + core
        for half in range(2):
            pltpu.make_async_copy(
                w_up.at[half, j, core],
                w.at[pl.ds(pl.multiple_of(j * 256 + half * DIM, DIM), DIM)], w_sem.at[j]).start()
        pltpu.make_async_copy(
            q_nope.at[:, columns(head)], qd.at[j, own_rows, pl.ds(0, DIM)], head_sem.at[j]).start()
        pltpu.make_async_copy(
            q_rope.at[:, columns(j)], qd.at[j, own_rows, pl.ds(DIM, DIM)], head_sem.at[j]).start()
        pltpu.make_async_copy(
            dout.at[:, columns(head)], qd.at[j, own_rows, pl.ds(2 * DIM, DIM)], head_sem.at[j]).start()
        return 0

    lax.fori_loop(0, PAIRS, load_head, 0)

    barrier = pltpu.get_barrier_semaphore()

    def greet(device):
        pl.semaphore_signal(barrier, inc=1, device_id=device, device_id_type=pl.DeviceIdType.MESH)

    for device in (sibling, after, before, x_one, x_two, y_one, y_two):
        greet(device)
    for step in range(1, PAIRS):
        greet(place(x_hi, x_lo, y_hi, y_lo, lax.rem(z + step, PAIRS)))
    pl.semaphore_wait(barrier, 6 + PAIRS)

    lat_next = remote(latent, lat.at[lat_rows(core)], lat_send.at[0], lat_recv.at[0], after)
    rope_next = remote(rope_key, ropes.at[core], lat_send.at[1], lat_recv.at[1], after)
    lat_sib = remote(latent, lat.at[lat_rows(2 + core)], lat_send.at[2], lat_recv.at[2], sibling)
    rope_sib = remote(rope_key, ropes.at[2 + core], lat_send.at[3], lat_recv.at[3], sibling)
    lat_fwd = remote(lat.at[lat_rows(core)], lat.at[lat_rows(core)], lat_send.at[4], lat_recv.at[4], sibling)
    rope_fwd = remote(ropes.at[core], ropes.at[core], lat_send.at[5], lat_recv.at[5], sibling)
    for copy in (lat_next, rope_next, lat_sib, rope_sib):
        copy.start()

    def send_head(j, _):
        head = 2 * j + other
        remote(q_nope.at[:, columns(head)], qd.at[j, own_rows, pl.ds(0, DIM)],
               q_send.at[j], q_recv.at[j], sibling).start()
        remote(q_rope.at[:, columns(j)], qd.at[j, own_rows, pl.ds(DIM, DIM)],
               q_send.at[j], q_recv.at[j], sibling).start()
        remote(dout.at[:, columns(head)], qd.at[j, own_rows, pl.ds(2 * DIM, DIM)],
               q_send.at[j], q_recv.at[j], sibling).start()
        return 0

    lax.fori_loop(0, PAIRS, send_head, 0)

    for copy in doc_copies:
        copy.wait()
    row = doc_row[...].astype(F32)
    key_docs = jnp.transpose(jnp.broadcast_to(row, (DIM, 512)))
    key_docs = jnp.concatenate([key_docs, key_docs], axis=1)
    query_docs = jnp.broadcast_to(row[:, 256:], (512, 256))
    key_at = lax.broadcasted_iota(jnp.int32, (512, 256), 0)
    query_at = lax.broadcasted_iota(jnp.int32, (512, 256), 1)
    first_key = jnp.where(chip == 0, 256, 0)
    seen = (
        (key_at <= query_at + 256) & (key_at > query_at) & (key_at >= first_key)
        & (key_docs == query_docs)
    )
    bias[...] = jnp.where(seen, 0.0, -jnp.inf)
    rope_grad[...] = jnp.zeros_like(rope_grad)

    lat_next.wait_recv()
    lat_fwd.start()
    rope_next.wait_recv()
    rope_fwd.start()
    pltpu.make_async_copy(latent, lat.at[lat_rows(2 + core)], local_sem.at[0]).wait()
    pltpu.make_async_copy(rope_key, ropes.at[2 + core], local_sem.at[1]).wait()
    lat_sib.wait_recv()
    rope_sib.wait_recv()
    lat_fwd.wait_recv()
    rope_fwd.wait_recv()

    spread_row = lax.broadcasted_iota(jnp.int32, (ROPE, DIM), 0)
    spread_col = lax.broadcasted_iota(jnp.int32, (ROPE, DIM), 1)
    spread = jnp.where(spread_col == spread_row + core * ROPE, 1.0, 0.0).astype(BF16)
    for slot in range(4):
        rope_tile[slot * BLOCK:(slot + 1) * BLOCK] = nn(ropes[slot], spread).astype(BF16)

    def attend(j):
        pltpu.make_async_copy(qd.at[j, own_rows], qd.at[j, own_rows], head_sem.at[j]).wait()
        remote(qd.at[j, sib_rows], qd.at[j, sib_rows], q_send.at[j], q_recv.at[j], sibling).wait_recv()
        w_rows = pl.ds(pl.multiple_of(j * 256, 256), 256)
        pltpu.make_async_copy(w.at[w_rows], w.at[w_rows], w_sem.at[j]).wait()
        q_cat = qd[j, :, :256]
        grads = qd[j, :, 256:]
        kv = nt(lat[...], w[w_rows]).astype(BF16)
        k_cat = jnp.concatenate([kv[:, :DIM], rope_tile[...]], axis=1)
        values = kv[:, DIM:]
        scores = nt(k_cat, q_cat) * (SCALE * LOG2E) + bias[...]
        grad_probs = nt(values, grads)
        highest = jnp.max(scores, axis=0, keepdims=True)
        weights = jnp.exp2(scores - highest)
        inverse = 1.0 / jnp.sum(weights, axis=0, keepdims=True)
        probs = weights * inverse
        delta = jnp.sum(probs * grad_probs, axis=0, keepdims=True)
        probs_low = probs.astype(BF16)
        grad_scores = (probs * ((grad_probs - delta) * SCALE)).astype(BF16)
        key_grad = nn(grad_scores, q_cat)
        value_grad = nn(probs_low, grads)
        rope_grad[...] += key_grad[:, DIM:]
        both = jnp.concatenate([key_grad[:, :DIM].astype(BF16), value_grad.astype(BF16)], axis=1)
        gkv[:, pl.ds(pl.multiple_of(j * 256, 256), 256)] = both
        up = tn(both, lat[...]).astype(BF16)
        for xh in range(2):
            for xl in range(2):
                for yy in range(4):
                    yh, yl = yy // 2, yy % 2
                    start = xl * DIM + yy * 32 + xh * 16
                    x_places = ((xh + xl) % 2 * 2 + xh, xh * 2 + xl)
                    y_places = ((yh + yl) % 2 * 2 + yh, yh * 2 + yl)
                    for quarter in range(4):
                        letter = quarter % 2
                        a, b = x_places[letter], y_places[letter]
                        if quarter >= 2:
                            a, b = b, a
                        part[j, quarter, a, b] = up[start:start + 16, quarter * DIM:(quarter + 1) * DIM]
        for quarter in range(4):
            group, _, partner, _ = first[quarter]
            remote(part.at[j, quarter, pl.ds((1 - group) * 2, 2)], in1.at[j, quarter],
                   rs_send.at[0, j], rs_recv.at[0, j], partner).start()
        qg[j] = tn(grad_scores, k_cat).astype(BF16)
        head = 2 * j + core
        remote(qg.at[j, sib_rows, pl.ds(0, DIM)], qn_out.at[:, columns(head)],
               g_send.at[0, j], g_recv.at[0, j], sibling).start()
        remote(qg.at[j, sib_rows, pl.ds(DIM, DIM)], qr_in.at[j],
               g_send.at[1, j], g_recv.at[1, j], sibling).start()
        pltpu.make_async_copy(
            qg.at[j, own_rows, pl.ds(0, DIM)], qn_out.at[:, columns(head)], qn_sem.at[j]).start()

    def arrived(buffer, step, j):
        remote(buffer.at[j], buffer.at[j], rs_send.at[step, j], rs_recv.at[step, j], sibling).wait_recv()

    def step_two(j):
        arrived(in1, 0, j)
        for quarter in range(4):
            group, low, _, partner = first[quarter]
            out2[j, quarter] = (
                part[j, quarter, group * 2 + 1 - low].astype(F32) + in1[j, quarter, 1 - low].astype(F32)
            ).astype(BF16)
            remote(out2.at[j, quarter], in2.at[j, quarter], rs_send.at[1, j], rs_recv.at[1, j], partner).start()

    def step_three(j):
        arrived(in2, 1, j)
        for quarter in range(4):
            group, low, _, _ = first[quarter]
            total[j, quarter] = (
                part[j, quarter, group * 2 + low].astype(F32)
                + in1[j, quarter, low].astype(F32) + in2[j, quarter].astype(F32)
            )
            group, _, partner, _ = second[quarter]
            out3[j, quarter] = total[j, quarter, pl.ds((1 - group) * 2, 2)].astype(BF16)
            remote(out3.at[j, quarter], in3.at[j, quarter], rs_send.at[2, j], rs_recv.at[2, j], partner).start()

    def step_four(j):
        arrived(in3, 2, j)
        for quarter in range(4):
            group, low, _, partner = second[quarter]
            out4[j, quarter] = (
                total[j, quarter, group * 2 + 1 - low] + in3[j, quarter, 1 - low].astype(F32)
            ).astype(BF16)
            remote(out4.at[j, quarter], in4.at[j, quarter], rs_send.at[3, j], rs_recv.at[3, j], partner).start()

    def step_five(j):
        arrived(in4, 3, j)
        for quarter in range(4):
            group, low, _, _ = second[quarter]
            summed = (
                total[j, quarter, group * 2 + low]
                + in3[j, quarter, low].astype(F32) + in4[j, quarter].astype(F32)
            )
            zf[j, :, quarter * DIM:(quarter + 1) * DIM] = summed
            zb[j, :, quarter * DIM:(quarter + 1) * DIM] = summed.astype(BF16)

        @pl.when(j != z)
        def _():
            remote(zb.at[j], zin.at[z], z_send.at[j], z_recv.at[z],
                   place(x_hi, x_lo, y_hi, y_lo, j)).start()

    lg_block = remote(lgs.at[0], lgr.at[0], lg_send.at[0], lg_recv.at[0], sibling)
    lg_own = remote(lgs.at[1], lgr.at[1], lg_send.at[1], lg_recv.at[1], sibling)
    lg_back = remote(lgs.at[2], lgr.at[2], lg_send.at[2], lg_recv.at[2], before)

    def project():
        lane = lax.broadcasted_iota(jnp.int32, (BLOCK, DIM), 1)
        mine = (lane >= core * ROPE) & (lane < (core + 1) * ROPE)
        for slot in range(4):
            rows = slice(slot * BLOCK, (slot + 1) * BLOCK)
            lgf[slot, :, :LATENT] = nn(gkv[rows], w[...])
            lgf[slot, :, LATENT:] = jnp.where(mine, rope_grad[rows], 0.0)
            if slot == 1:
                lgs[0] = lgf[other].astype(BF16)
                lg_block.start()
        lgs[1] = lgf[2 + other].astype(BF16)
        lg_own.start()

    def combine():
        lg_block.wait_recv()
        lgs[2] = (lgf[core] + lgr[0].astype(F32)).astype(BF16)
        lg_back.start()

    def turn(i, _):
        pl.when(i < PAIRS)(lambda: attend(i))
        pl.when(i == PAIRS)(project)
        for number, step in enumerate((step_two, step_three, step_four, step_five)):
            j = i - LAG * (number + 1)
            pl.when((j >= 0) & (j < PAIRS))(functools.partial(step, j))
        pl.when(i == PAIRS)(combine)
        return 0

    lax.fori_loop(0, PAIRS + LAG * STEPS, turn, 0)

    def finish_rope(j, _):
        remote(qr_in.at[j], qr_in.at[j], g_send.at[1, j], g_recv.at[1, j], sibling).wait_recv()
        qr_out[:, columns(j)] = qg[j, own_rows, DIM:] + qr_in[j]
        return 0

    lax.fori_loop(0, PAIRS, finish_rope, 0)
    lg_own.wait_recv()
    lg_back.wait_recv()
    grads = lgf[2 + core] + lgr[1].astype(F32) + lgr[2].astype(F32)
    lat_out[...] = grads[:, :LATENT]
    tile = grads[:, LATENT:]
    rope_out[...] = (tile + pltpu.roll(tile, ROPE, 1))[:, :ROPE]

    up_out[...] = zf[z]

    def add_plane(step, _):
        source = lax.rem(z + step, PAIRS)
        remote(zin.at[source], zin.at[source], z_send.at[source], z_recv.at[source], sibling).wait_recv()
        up_out[...] += zin[source].astype(F32)
        return 0

    lax.fori_loop(1, PAIRS, add_plane, 0)

    for copy in (lat_next, rope_next, lat_sib, rope_sib, lat_fwd, rope_fwd, lg_block, lg_own, lg_back):
        copy.wait_send()

    def ended(j, _):
        remote(qd.at[j, sib_rows], qd.at[j, sib_rows], q_send.at[j], q_recv.at[j], sibling).wait_send()
        head = 2 * j + other
        remote(qg.at[j, sib_rows, pl.ds(0, DIM)], qn_out.at[:, columns(head)],
               g_send.at[0, j], g_recv.at[0, j], sibling).wait()
        remote(qr_in.at[j], qr_in.at[j], g_send.at[1, j], g_recv.at[1, j], sibling).wait_send()
        pltpu.make_async_copy(
            qg.at[j, own_rows, pl.ds(0, DIM)], qn_out.at[:, columns(2 * j + core)], qn_sem.at[j]).wait()
        for step, buffer in enumerate((in1, in2, in3, in4)):
            remote(buffer.at[j], buffer.at[j], rs_send.at[step, j], rs_recv.at[step, j], sibling).wait_send()

        @pl.when(j != z)
        def _():
            remote(zb.at[j], zb.at[j], z_send.at[j], z_recv.at[j], sibling).wait_send()

        return 0

    lax.fori_loop(0, PAIRS, ended, 0)


def fused(q_nope, q_rope, dout, latent, rope_key, docs, w_up):
    any_space = pl.BlockSpec(memory_space=pl.ANY)
    vmem = pl.BlockSpec(memory_space=pltpu.VMEM)
    dma = pltpu.SemaphoreType.DMA
    scratch = [
        pltpu.VMEM((512, LATENT), BF16),
        pltpu.VMEM((4, BLOCK, ROPE), BF16),
        pltpu.VMEM((512, DIM), BF16),
        pltpu.VMEM((1, 512), jnp.int32),
        pltpu.VMEM((512, 256), F32),
        pltpu.VMEM((PAIRS * 256, LATENT), BF16),
        pltpu.VMEM((PAIRS, 256, 3 * DIM), BF16),
        pltpu.VMEM((PAIRS, 256, 256), BF16),
        pltpu.VMEM((PAIRS, BLOCK, DIM), BF16),
        pltpu.VMEM((512, PAIRS * 256), BF16),
        pltpu.VMEM((512, DIM), F32),
        pltpu.VMEM((4, BLOCK, LATENT + DIM), F32),
        pltpu.VMEM((3, BLOCK, LATENT + DIM), BF16),
        pltpu.VMEM((3, BLOCK, LATENT + DIM), BF16),
        pltpu.VMEM((PAIRS, 4, 4, 4, 16, DIM), BF16),
        pltpu.VMEM((PAIRS, 4, 2, 4, 16, DIM), BF16),
        pltpu.VMEM((PAIRS, 4, 4, 16, DIM), BF16),
        pltpu.VMEM((PAIRS, 4, 4, 16, DIM), BF16),
        pltpu.VMEM((PAIRS, 4, 4, 16, DIM), F32),
        pltpu.VMEM((PAIRS, 4, 2, 16, DIM), BF16),
        pltpu.VMEM((PAIRS, 4, 2, 16, DIM), BF16),
        pltpu.VMEM((PAIRS, 4, 16, DIM), BF16),
        pltpu.VMEM((PAIRS, 4, 16, DIM), BF16),
        pltpu.VMEM((PAIRS, 16, LATENT), F32),
        pltpu.VMEM((PAIRS, 16, LATENT), BF16),
        pltpu.VMEM((PAIRS, 16, LATENT), BF16),
        dma((4,)), dma((PAIRS,)), dma((PAIRS,)), dma((PAIRS,)),
        dma((6,)), dma((6,)), dma((PAIRS,)), dma((PAIRS,)),
        dma((2, PAIRS)), dma((2, PAIRS)), dma((3,)), dma((3,)),
        dma((STEPS, PAIRS)), dma((STEPS, PAIRS)), dma((PAIRS,)), dma((PAIRS,)),
    ]
    return pl.pallas_call(
        kernel,
        out_shape=(
            jax.ShapeDtypeStruct((BLOCK, 2048), BF16),
            jax.ShapeDtypeStruct((BLOCK, 1024), BF16),
            jax.ShapeDtypeStruct((BLOCK, LATENT), F32),
            jax.ShapeDtypeStruct((BLOCK, ROPE), F32),
            jax.ShapeDtypeStruct((16, LATENT), F32),
        ),
        in_specs=[any_space] * 7,
        out_specs=(any_space, vmem, vmem, vmem, vmem),
        scratch_shapes=scratch,
        compiler_params=pltpu.CompilerParams(
            collective_id=0, has_side_effects=True, vmem_limit_bytes=48 * 1024 * 1024
        ),
        name="latent_attention_grads",
    )(q_nope, q_rope, dout, latent, rope_key, docs, w_up)


def body(q_nope, q_rope, dout, latent, rope_key, doc_ids, w_up):
    outs = fused(
        q_nope[0], q_rope[0], dout[0], latent[0], rope_key[0], doc_ids,
        w_up.reshape(2, PAIRS, 2, DIM, LATENT),
    )
    return tuple(out[None] for out in outs[:4]) + (outs[4],)


def solution(mesh):
    return jax.shard_map(
        body,
        mesh=mesh,
        in_specs=(
            P("dp", "ctx", None),
            P("dp", "ctx", None),
            P("dp", "ctx", None),
            P("dp", "ctx", None),
            P("dp", "ctx", None),
            P("dp", None),
            P(),
        ),
        out_specs=(
            P("dp", "ctx", None),
            P("dp", "ctx", None),
            P("dp", "ctx", None),
            P("dp", "ctx", None),
            P(("ctx", "dp"), None),
        ),
        check_vma=False,
    )
```

time: 1440 us -> 54.2 us (0.04)
  the two profiles are of different devices: /device:TPU:128 before, /device:TPU:224 now
where the time goes in v1:
time: 54.2 us; the launch traced here: 53.9 us
  Pallas kernels  44.2 us (82%)
  local copies, waits for them, and re-layouts  8.99 us (17%)
  between operations  0.66 us (1%)
    pallas_call x1, Pallas kernels, fused(): pl.pallas_call(kernel, out_shape=(jax.ShapeDtypeStruct((BLOCK, 2048), BF1...  44.2 us
    unnamed x16, local copies, waits for them, and re-layouts  8.99 us

profile of v1, /device:TPU:224, one launch (start us, length us, event | category | flops | bytes accessed | tf_op | source)
XLA Modules:
  0.0 53.9 jit_solution(7863950503850880391)
XLA Ops:
  0.6 0.8 %copy.12 = bf16[1,128,64]{2,1,0:T(8,128)(2,1)S(1)} copy(bf16[1,128,64]{1,2,0:T(8,128)(2,1)} %param.11) | data formatting | bytes 32768 | tf_op args[4]
  1.5 0.0 copy-start
  1.5 1.0 %copy-done = bf16[1,128,2048]{2,1,0:T(8,128)(2,1)S(1)} copy-done((bf16[1,128,2048]{2,1,0:T(8,128)(2,1)S(1)}, bf16[1,128,2048]{2,1,0:T(8,128)(2,1)}, u32[]{:S(2)}) %copy-start) | copy-done | bytes 524312
  2.5 0.0 copy-start.1
  2.5 1.0 %copy-done.1 = bf16[1,128,2048]{2,1,0:T(8,128)(2,1)S(1)} copy-done((bf16[1,128,2048]{2,1,0:T(8,128)(2,1)S(1)}, bf16[1,128,2048]{2,1,0:T(8,128)(2,1)}, u32[]{:S(2)}) %copy-start.1) | copy-done | bytes 524312
  3.6 0.0 copy-start.2
  3.6 0.9 %copy-done.2 = bf16[1,128,1024]{2,1,0:T(8,128)(2,1)S(1)} copy-done((bf16[1,128,1024]{2,1,0:T(8,128)(2,1)S(1)}, bf16[1,128,1024]{2,1,0:T(8,128)(2,1)}, u32[]{:S(2)}) %copy-start.2) | copy-done | bytes 262168
  4.5 0.0 copy-start.3
  4.5 0.9 %copy-done.3 = bf16[1,128,512]{2,1,0:T(8,128)(2,1)S(1)} copy-done((bf16[1,128,512]{2,1,0:T(8,128)(2,1)S(1)}, bf16[1,128,512]{2,1,0:T(8,128)(2,1)}, u32[]{:S(2)}) %copy-start.3) | copy-done | bytes 131096
  5.4 0.0 copy-start.4
  5.4 0.7 %copy-done.4 = s32[1,4096]{1,0:T(1,128)S(1)} copy-done((s32[1,4096]{1,0:T(1,128)S(1)}, s32[1,4096]{1,0:T(1,128)}, u32[]{:S(2)}) %copy-start.4) | copy-done | bytes 16408
  6.1 44.2 %latent_attention_grads.1 = (bf16[128,2048]{1,0:T(8,128)(2,1)S(1)}, bf16[128,1024]{1,0:T(8,128)(2,1)S(1)}, f32[128,512]{1,0:T(8,128)S(1)}, f32[128,64]{1,0:T(8,128)S(1)}, f32[16,512]{1,0:T(8,128)S(1)}) custom-call(bf16[128,2048]{1,0:T(8,128)(2,1)S(1)} %bitcast.11, bf16[128,1024]{1,0:T(8,128)(2,1)S(1)} %bitcast.13, bf16[128,2048]{1,0:T(8,128)(2,1)S(1)} %bitcast.12, ...), custom_call_target="tpu_custom_call" | custom-call | tf_op jit(solution)/shard_map/latent_attention_grads/pallas_call | solution.py:399
  50.4 0.7 %copy.13 = f32[1,128,64]{1,2,0:T(8,128)} copy(f32[1,128,64]{2,1,0:T(8,128)S(1)} %bitcast.18) | data formatting | bytes 65536
  51.1 0.8 %copy.18 = bf16[1,128,2048]{2,1,0:T(8,128)(2,1)} copy(bf16[1,128,2048]{2,1,0:T(8,128)(2,1)S(1)} %bitcast.10) | data formatting | bytes 1048576
  51.8 0.7 %copy.19 = bf16[1,128,1024]{2,1,0:T(8,128)(2,1)} copy(bf16[1,128,1024]{2,1,0:T(8,128)(2,1)S(1)} %bitcast.15) | data formatting | bytes 524288
  52.6 0.7 %copy.20 = f32[1,128,512]{2,1,0:T(8,128)} copy(f32[1,128,512]{2,1,0:T(8,128)S(1)} %bitcast.14) | data formatting | bytes 524288
  53.3 0.6 %copy.21 = f32[16,512]{1,0:T(8,128)} copy(f32[16,512]{1,0:T(8,128)S(1)} %get-tuple-element.29) | data formatting | bytes 65536
Async XLA Ops:
  1.5 1.1 %copy-start = (bf16[1,128,2048]{2,1,0:T(8,128)(2,1)S(1)}, bf16[1,128,2048]{2,1,0:T(8,128)(2,1)}, u32[]{:S(2)}) copy-start(bf16[1,128,2048]{2,1,0:T(8,128)(2,1)} %param.7) | copy-start | bytes 1572868
  2.5 1.0 %copy-start.1 = (bf16[1,128,2048]{2,1,0:T(8,128)(2,1)S(1)}, bf16[1,128,2048]{2,1,0:T(8,128)(2,1)}, u32[]{:S(2)}) copy-start(bf16[1,128,2048]{2,1,0:T(8,128)(2,1)} %param.9) | copy-start | bytes 1572868
  3.6 0.9 %copy-start.2 = (bf16[1,128,1024]{2,1,0:T(8,128)(2,1)S(1)}, bf16[1,128,1024]{2,1,0:T(8,128)(2,1)}, u32[]{:S(2)}) copy-start(bf16[1,128,1024]{2,1,0:T(8,128)(2,1)} %param.8) | copy-start | bytes 786436
  4.5 0.9 %copy-start.3 = (bf16[1,128,512]{2,1,0:T(8,128)(2,1)S(1)}, bf16[1,128,512]{2,1,0:T(8,128)(2,1)}, u32[]{:S(2)}) copy-start(bf16[1,128,512]{2,1,0:T(8,128)(2,1)} %param.10) | copy-start | bytes 393220
  5.4 0.7 %copy-start.4 = (s32[1,4096]{1,0:T(1,128)S(1)}, s32[1,4096]{1,0:T(1,128)}, u32[]{:S(2)}) copy-start(s32[1,4096]{1,0:T(1,128)} %docs.1) | copy-start | bytes 49156

commit v2 on v1

v2 whole, which is shorter than its diff:
```python
import functools

import jax
import jax.numpy as jnp
from jax import lax
from jax.experimental import pallas as pl
from jax.experimental.pallas import tpu as pltpu
from jax.sharding import PartitionSpec as P

LATENT = 512
ROPE = 64
DIM = 128
BLOCK = 128
PAIRS = 8
CHIPS = 16
CHUNKS = 4
CHUNK = BLOCK // CHUNKS
VMEM_BYTES = 40 * 1024 * 1024
STEPS = 2
SCALE = float(DIM + ROPE) ** -0.5
LOG2E = 1.4426950408889634
F32 = jnp.float32
BF16 = jnp.bfloat16


def nt(a, b):
    return lax.dot_general(a, b, (((1,), (1,)), ((), ())), preferred_element_type=F32)


def nn(a, b):
    return lax.dot_general(a, b, (((1,), (0,)), ((), ())), preferred_element_type=F32)


def tn(a, b):
    return lax.dot_general(a, b, (((0,), (0,)), ((), ())), preferred_element_type=F32)


def offsets(turn):
    late = turn // 2
    return 3 + turn, (1 + 6 * turn) * (1 - late) + (6 - 2 * turn) * late


def kernel(
    q_nope, q_rope, dout, latent, rope_key, docs, w_up,
    qn_out, qr_out, lat_out, rope_out, up_out,
    lat, ropes, rope_tile, doc_row, bias, w, qd, qg, qr_in, gkv, rope_grad, lgf, lgs, lgr,
    kv_own, scores_own, products_own, grad_scores_kept, k_kept, part, in1, total, out2, in2, near_in, zf, zb, zin,
    local_sem, head_sem, w_sem,
    lat_send, lat_recv, q_send, q_recv, g_send, g_recv, lg_send, lg_recv,
    rs_send, rs_recv, z_send, z_recv, near_send, near_recv,
):
    ctx = lax.axis_index("ctx")
    dp = lax.axis_index("dp")
    core = lax.rem(ctx, 2)
    other = 1 - core
    chip = lax.div(ctx, 2)
    x_lo, z = lax.div(chip, PAIRS), lax.rem(chip, PAIRS)
    y, x_hi = lax.div(dp, 2), lax.rem(dp, 2)

    def at(ctx_index, dp_index):
        return {"ctx": ctx_index, "dp": dp_index}

    def place(xh, xl, yy, zz):
        return at((xl * PAIRS + zz) * 2 + core, yy * 2 + xh)

    sibling = at(chip * 2 + other, dp)
    after = at(lax.rem(chip + 1, CHIPS) * 2 + core, dp)
    before = at(lax.rem(chip + CHIPS - 1, CHIPS) * 2 + core, dp)
    x = x_hi * 2 + x_lo

    def x_on(step):
        to = lax.rem(x + step, 4)
        return place(lax.div(to, 2), lax.rem(to, 2), y, z)

    def y_on(step):
        return place(x_hi, x_lo, lax.rem(y + step, 4), z)

    above = place(x_hi, x_lo, y, lax.rem(z + 1, PAIRS))
    below = place(x_hi, x_lo, y, lax.rem(z + PAIRS - 1, PAIRS))
    first = ((x, x_on), (y, y_on))
    second = ((y, y_on), (x, x_on))

    own_rows = pl.ds(pl.multiple_of(core * BLOCK, BLOCK), BLOCK)
    sib_rows = pl.ds(pl.multiple_of(other * BLOCK, BLOCK), BLOCK)

    def lat_rows(slot):
        return pl.ds(pl.multiple_of(slot * BLOCK, BLOCK), BLOCK)

    def columns(index):
        return pl.ds(pl.multiple_of(index * DIM, DIM), DIM)

    def remote(src, dst, send, recv, device):
        return pltpu.make_async_remote_copy(
            src_ref=src, dst_ref=dst, send_sem=send, recv_sem=recv,
            device_id=device, device_id_type=pl.DeviceIdType.MESH,
        )

    barrier = pltpu.get_barrier_semaphore()

    def greet(device):
        pl.semaphore_signal(barrier, inc=1, device_id=device, device_id_type=pl.DeviceIdType.MESH)

    for device in (sibling, after, before):
        greet(device)
    for step in range(1, 4):
        greet(x_on(step))
        greet(y_on(step))
    for step in range(1, PAIRS):
        greet(place(x_hi, x_lo, y, lax.rem(z + step, PAIRS)))

    pltpu.make_async_copy(latent, lat.at[lat_rows(2 + core)], local_sem.at[0]).start()
    pltpu.make_async_copy(rope_key, ropes.at[2 + core], local_sem.at[1]).start()
    behind = lax.rem(chip + CHIPS - 1, CHIPS)
    doc_copies = (
        pltpu.make_async_copy(
            docs.at[:, pl.ds(pl.multiple_of(behind * 256, 256), 256)],
            doc_row.at[:, pl.ds(0, 256)], local_sem.at[2]),
        pltpu.make_async_copy(
            docs.at[:, pl.ds(pl.multiple_of(chip * 256, 256), 256)],
            doc_row.at[:, pl.ds(256, 256)], local_sem.at[3]),
    )
    for copy in doc_copies:
        copy.start()

    def load_head(j, _):
        head = 2 * j + core
        for half in range(2):
            pltpu.make_async_copy(
                w_up.at[half, j, core],
                w.at[pl.ds(pl.multiple_of(j * 256 + half * DIM, DIM), DIM)], w_sem.at[j]).start()
        pltpu.make_async_copy(
            q_nope.at[:, columns(head)], qd.at[j, own_rows, pl.ds(0, DIM)], head_sem.at[j]).start()
        pltpu.make_async_copy(
            q_rope.at[:, columns(j)], qd.at[j, own_rows, pl.ds(DIM, DIM)], head_sem.at[j]).start()
        pltpu.make_async_copy(
            dout.at[:, columns(head)], qd.at[j, own_rows, pl.ds(2 * DIM, DIM)], head_sem.at[j]).start()
        return 0

    lax.fori_loop(0, PAIRS, load_head, 0)

    pl.semaphore_wait(barrier, 8 + PAIRS)


    def lat_chunk(slot, chunk):
        return pl.ds(pl.multiple_of(slot * BLOCK + chunk * CHUNK, CHUNK), CHUNK)

    rope_next = remote(rope_key, ropes.at[core], lat_send.at[0], lat_recv.at[0], after)
    rope_sib = remote(rope_key, ropes.at[2 + core], lat_send.at[1], lat_recv.at[1], sibling)
    rope_fwd = remote(ropes.at[core], ropes.at[core], lat_send.at[2], lat_recv.at[2], sibling)
    lat_sib = remote(latent, lat.at[lat_rows(2 + core)], lat_send.at[3], lat_recv.at[3], sibling)
    lat_next = [
        remote(latent.at[pl.ds(n * CHUNK, CHUNK)], lat.at[lat_chunk(core, n)],
               lat_send.at[4 + n], lat_recv.at[4 + n], after)
        for n in range(CHUNKS)
    ]
    lat_fwd = [
        remote(lat.at[lat_chunk(core, n)], lat.at[lat_chunk(core, n)],
               lat_send.at[4 + CHUNKS + n], lat_recv.at[4 + CHUNKS + n], sibling)
        for n in range(CHUNKS)
    ]
    for copy in (rope_next, *lat_next, lat_sib, rope_sib):
        copy.start()

    def send_head(j, _):
        head = 2 * j + other
        remote(q_nope.at[:, columns(head)], qd.at[j, own_rows, pl.ds(0, DIM)],
               q_send.at[j], q_recv.at[j], sibling).start()
        remote(q_rope.at[:, columns(j)], qd.at[j, own_rows, pl.ds(DIM, DIM)],
               q_send.at[j], q_recv.at[j], sibling).start()
        remote(dout.at[:, columns(head)], qd.at[j, own_rows, pl.ds(2 * DIM, DIM)],
               q_send.at[j], q_recv.at[j], sibling).start()
        return 0

    lax.fori_loop(0, PAIRS, send_head, 0)

    for copy in doc_copies:
        copy.wait()
    row = doc_row[...].astype(F32)
    key_docs = jnp.transpose(jnp.broadcast_to(row, (DIM, 512)))
    key_docs = jnp.concatenate([key_docs, key_docs], axis=1)
    query_docs = jnp.broadcast_to(row[:, 256:], (512, 256))
    key_at = lax.broadcasted_iota(jnp.int32, (512, 256), 0)
    query_at = lax.broadcasted_iota(jnp.int32, (512, 256), 1)
    first_key = jnp.where(chip == 0, 256, 0)
    seen = (
        (key_at <= query_at + 256) & (key_at > query_at) & (key_at >= first_key)
        & (key_docs == query_docs)
    )
    bias[...] = jnp.where(seen, 0.0, -jnp.inf)
    rope_grad[...] = jnp.zeros_like(rope_grad)

    pltpu.make_async_copy(latent, lat.at[lat_rows(2 + core)], local_sem.at[0]).wait()
    pltpu.make_async_copy(rope_key, ropes.at[2 + core], local_sem.at[1]).wait()
    lat_sib.wait_recv()
    rope_sib.wait_recv()

    spread_row = lax.broadcasted_iota(jnp.int32, (ROPE, DIM), 0)
    spread_col = lax.broadcasted_iota(jnp.int32, (ROPE, DIM), 1)
    spread = jnp.where(spread_col == spread_row + core * ROPE, 1.0, 0.0).astype(BF16)

    def spread_rope(slot):
        rope_tile[slot * BLOCK:(slot + 1) * BLOCK] = tn(ropes[slot], spread).astype(BF16)

    spread_rope(2)
    spread_rope(3)

    def wait_weights(j, _):
        w_rows = pl.ds(pl.multiple_of(j * 256, 256), 256)
        pltpu.make_async_copy(w.at[w_rows], w.at[w_rows], w_sem.at[j]).wait()
        return 0

    lax.fori_loop(0, PAIRS, wait_weights, 0)
    kv_own[...] = nt(lat[256:], w[...]).astype(BF16)

    def own_keys(i, _):
        heads = (2 * i, 2 * i + 1)
        for j in heads:
            pltpu.make_async_copy(qd.at[j, own_rows], qd.at[j, own_rows], head_sem.at[j]).wait()
            remote(qd.at[j, sib_rows], qd.at[j, sib_rows], q_send.at[j], q_recv.at[j], sibling).wait_recv()
        kv = kv_own[:, pl.ds(pl.multiple_of(i * 512, 512), 512)]
        rope = rope_tile[256:]
        keys = [jnp.concatenate([kv[:, n * 256:n * 256 + DIM], rope], axis=1) for n in range(2)]
        scores = [nt(keys[n], qd[j, :, :256]) for n, j in enumerate(heads)]
        products = [nt(kv[:, n * 256 + DIM:(n + 1) * 256], qd[j, :, 256:]) for n, j in enumerate(heads)]
        for n, j in enumerate(heads):
            k_kept[j, 256:] = keys[n]
            scores_own[j] = scores[n] * (SCALE * LOG2E) + bias[256:]
            products_own[j] = products[n]
        return 0

    lax.fori_loop(0, PAIRS // 2, own_keys, 0)
    rope_next.wait_recv()
    rope_fwd.start()
    for arriving, onward in zip(lat_next, lat_fwd):
        arriving.wait_recv()
        onward.start()
    rope_fwd.wait_recv()
    for copy in lat_fwd:
        copy.wait_recv()
    spread_rope(0)
    spread_rope(1)

    def pair_on(offset):
        return lax.rem(z + offset, PAIRS)

    def send_first(j):
        for half, (index, on) in enumerate(first):
            for step in range(1, 4):
                remote(part.at[j, half, lax.rem(index + step, 4)], in1.at[j, half, step - 1],
                       rs_send.at[0, j], rs_recv.at[0, j], on(step)).start()

    def attend(i, _):
        heads = [pair_on(offset) for offset in offsets(i)]
        kv = [nt(lat[:256], w[pl.ds(pl.multiple_of(j * 256, 256), 256)]).astype(BF16) for j in heads]
        rope = rope_tile[:256]
        keys = [jnp.concatenate([kv[n][:, :DIM], rope], axis=1) for n in range(2)]
        scores = [nt(keys[n], qd[j, :, :256]) for n, j in enumerate(heads)]
        products = [nt(kv[n][:, DIM:], qd[j, :, 256:]) for n, j in enumerate(heads)]
        probs_low, grad_scores = [], []
        for n, j in enumerate(heads):
            k_kept[j, :256] = keys[n]
            score = jnp.concatenate([scores[n] * (SCALE * LOG2E) + bias[:256], scores_own[j]], axis=0)
            grad_probs = jnp.concatenate([products[n], products_own[j]], axis=0)
            weights = jnp.exp2(score - jnp.max(score, axis=0, keepdims=True))
            probs = weights * (1.0 / jnp.sum(weights, axis=0, keepdims=True))
            delta = jnp.sum(probs * grad_probs, axis=0, keepdims=True)
            probs_low.append(probs.astype(BF16))
            grad_scores.append((probs * ((grad_probs - delta) * SCALE)).astype(BF16))
        rope_sum = rope_grad[...]
        both = []
        for n, j in enumerate(heads):
            key_grad = nn(grad_scores[n], qd[j, :, :256])
            value_grad = nn(probs_low[n], qd[j, :, 256:])
            rope_sum = rope_sum + key_grad[:, DIM:]
            both.append(jnp.concatenate([key_grad[:, :DIM].astype(BF16), value_grad.astype(BF16)], axis=1))
        rope_grad[...] = rope_sum
        for n, j in enumerate(heads):
            gkv[:, pl.ds(pl.multiple_of(j * 256, 256), 256)] = both[n]
        ups = [tn(both[n], lat[...]).astype(BF16) for n in range(2)]
        for n, j in enumerate(heads):
            for to_x in range(4):
                for to_y in range(4):
                    start = to_x % 2 * DIM + to_y * 32 + to_x // 2 * 16
                    part[j, 0, to_x, to_y] = ups[n][start:start + 16, :256]
                    part[j, 1, to_y, to_x] = ups[n][start:start + 16, 256:]
        send_first(heads[0])
        pl.when(i == 0)(lambda: remote(
            part.at[heads[1]], near_in.at[0], near_send.at[0], near_recv.at[0], above).start())
        pl.when(i == 1)(lambda: remote(
            part.at[heads[1]], near_in.at[1], near_send.at[1], near_recv.at[1], below).start())
        pl.when(i == 2)(lambda: send_first(heads[1]))
        for n, j in enumerate(heads):
            grad_scores_kept[j] = grad_scores[n]
        return 0

    def merge_near():
        for n, device in enumerate((above, below)):
            remote(near_in.at[n], near_in.at[n], near_send.at[n], near_recv.at[n], device).wait_recv()

        def merge_part(index, _):
            for half in range(2):
                part[z, half, index] = (
                    part[z, half, index].astype(F32)
                    + near_in[0, half, index].astype(F32) + near_in[1, half, index].astype(F32)
                ).astype(BF16)
            return 0

        lax.fori_loop(0, 4, merge_part, 0)
        send_first(z)

    def query_grads(i, _):
        heads = (2 * i, 2 * i + 1)
        grads = [tn(grad_scores_kept[j], k_kept[j]).astype(BF16) for j in heads]
        for n, j in enumerate(heads):
            qg[j] = grads[n]
            head = 2 * j + core
            remote(qg.at[j, sib_rows, pl.ds(0, DIM)], qn_out.at[:, columns(head)],
                   g_send.at[0, j], g_recv.at[0, j], sibling).start()
            remote(qg.at[j, sib_rows, pl.ds(DIM, DIM)], qr_in.at[j],
                   g_send.at[1, j], g_recv.at[1, j], sibling).start()
            qn_out[:, columns(head)] = qg[j, own_rows, :DIM]
        return 0

    def arrived(buffer, step, j):
        remote(buffer.at[j], buffer.at[j], rs_send.at[step, j], rs_recv.at[step, j], sibling).wait_recv()

    def step_two(j):
        arrived(in1, 0, j)
        for half, (index, on) in enumerate(second):
            own, _ = first[half]
            summed = part[j, half, own].astype(F32)
            for step in range(3):
                summed = summed + in1[j, half, step].astype(F32)
            total[j, half] = summed
            out2[j, half] = summed.astype(BF16)
            for step in range(1, 4):
                remote(out2.at[j, half, lax.rem(index + step, 4)], in2.at[j, half, step - 1],
                       rs_send.at[1, j], rs_recv.at[1, j], on(step)).start()

    def step_three(j):
        arrived(in2, 1, j)
        for half, (own, _) in enumerate(second):
            summed = total[j, half, own]
            for step in range(3):
                summed = summed + in2[j, half, step].astype(F32)
            zf[j, :, half * 256:(half + 1) * 256] = summed
            zb[j, :, half * 256:(half + 1) * 256] = summed.astype(BF16)

    def step_four(j):
        remote(zb.at[j], zin.at[z], z_send.at[j], z_recv.at[z], place(x_hi, x_lo, y, j)).start()

    lg_block = remote(lgs.at[0], lgr.at[0], lg_send.at[0], lg_recv.at[0], sibling)
    lg_own = remote(lgs.at[1], lgr.at[1], lg_send.at[1], lg_recv.at[1], sibling)
    lg_back = remote(lgs.at[2], lgr.at[2], lg_send.at[2], lg_recv.at[2], before)

    def project():
        lane = lax.broadcasted_iota(jnp.int32, (BLOCK, DIM), 1)
        mine = (lane >= core * ROPE) & (lane < (core + 1) * ROPE)
        for slot in range(4):
            rows = slice(slot * BLOCK, (slot + 1) * BLOCK)
            lgf[slot, :, :LATENT] = nn(gkv[rows], w[...])
            lgf[slot, :, LATENT:] = jnp.where(mine, rope_grad[rows], 0.0)
            if slot == 1:
                lgs[0] = lgf[other].astype(BF16)
                lg_block.start()
        lgs[1] = lgf[2 + other].astype(BF16)
        lg_own.start()

    def combine():
        lg_block.wait_recv()
        lgs[2] = (lgf[core] + lgr[0].astype(F32)).astype(BF16)
        lg_back.start()

    def finish_plane(offset):
        step_three(pair_on(offset))
        step_four(pair_on(offset))

    lax.fori_loop(0, PAIRS // 2, attend, 0)
    step_two(pair_on(3))
    project()
    step_two(pair_on(4))
    lax.fori_loop(0, 2, query_grads, 0)
    combine()
    step_two(pair_on(5))
    finish_plane(3)
    lax.fori_loop(2, 4, query_grads, 0)
    step_two(pair_on(2))
    merge_near()
    finish_plane(4)
    step_two(pair_on(6))
    finish_plane(5)
    finish_plane(2)

    def finish_head(j, _):
        head = 2 * j + other
        remote(qg.at[j, sib_rows, pl.ds(0, DIM)], qn_out.at[:, columns(head)],
               g_send.at[0, j], g_recv.at[0, j], sibling).wait()
        remote(qr_in.at[j], qr_in.at[j], g_send.at[1, j], g_recv.at[1, j], sibling).wait()
        qr_out[:, columns(j)] = qg[j, own_rows, DIM:] + qr_in[j]
        remote(qd.at[j, sib_rows], qd.at[j, sib_rows], q_send.at[j], q_recv.at[j], sibling).wait_send()
        return 0

    lax.fori_loop(0, PAIRS, finish_head, 0)
    for n, device in enumerate((above, below)):
        remote(near_in.at[n], near_in.at[n], near_send.at[n], near_recv.at[n], device).wait_send()
    lg_own.wait_recv()
    lg_back.wait_recv()
    grads = lgf[2 + core] + lgr[1].astype(F32) + lgr[2].astype(F32)
    lat_out[...] = grads[:, :LATENT]
    tile = grads[:, LATENT:]
    rope_out[...] = jnp.transpose(tile + pltpu.roll(tile, ROPE, 1))[:ROPE]
    for copy in (rope_next, *lat_next, lat_sib, rope_sib, *lat_fwd, rope_fwd, lg_block, lg_own, lg_back):
        copy.wait_send()

    step_two(z)
    finish_plane(6)
    step_three(z)
    up_out[...] = zf[z]

    def add_plane(step, _):
        source = lax.rem(z + step, PAIRS)
        remote(zin.at[source], zin.at[source], z_send.at[source], z_recv.at[source], sibling).wait_recv()
        up_out[...] += zin[source].astype(F32)
        return 0

    lax.fori_loop(2, PAIRS - 1, add_plane, 0)

    def sums_ended(step, _):
        j = pair_on(step)
        for number, buffer in enumerate((in1, in2)):
            remote(buffer.at[j], buffer.at[j], rs_send.at[number, j], rs_recv.at[number, j], sibling).wait_send()
        return 0

    def plane_ended(step, _):
        j = pair_on(step)
        remote(zb.at[j], zb.at[j], z_send.at[j], z_recv.at[j], sibling).wait_send()
        return sums_ended(step, 0)

    lax.fori_loop(2, PAIRS - 1, plane_ended, 0)
    sums_ended(0, 0)


def fused(*arrays):
    hbm = pl.BlockSpec(memory_space=pltpu.HBM)
    dma = pltpu.SemaphoreType.DMA
    scratch = [
        pltpu.VMEM((512, LATENT), BF16),
        pltpu.VMEM((4, ROPE, BLOCK), BF16),
        pltpu.VMEM((512, DIM), BF16),
        pltpu.VMEM((1, 512), jnp.int32),
        pltpu.VMEM((512, 256), F32),
        pltpu.VMEM((PAIRS * 256, LATENT), BF16),
        pltpu.VMEM((PAIRS, 256, 3 * DIM), BF16),
        pltpu.VMEM((PAIRS, 256, 256), BF16),
        pltpu.VMEM((PAIRS, BLOCK, DIM), BF16),
        pltpu.VMEM((512, PAIRS * 256), BF16),
        pltpu.VMEM((512, DIM), F32),
        pltpu.VMEM((4, BLOCK, LATENT + DIM), F32),
        pltpu.VMEM((3, BLOCK, LATENT + DIM), BF16),
        pltpu.VMEM((3, BLOCK, LATENT + DIM), BF16),
        pltpu.VMEM((256, PAIRS * 256), BF16),
        pltpu.VMEM((PAIRS, 256, 256), F32),
        pltpu.VMEM((PAIRS, 256, 256), F32),
        pltpu.VMEM((PAIRS, 512, 256), BF16),
        pltpu.VMEM((PAIRS, 512, 256), BF16),
        pltpu.VMEM((PAIRS, 2, 4, 4, 16, 256), BF16),
        pltpu.VMEM((PAIRS, 2, 3, 4, 16, 256), BF16),
        pltpu.VMEM((PAIRS, 2, 4, 16, 256), F32),
        pltpu.VMEM((PAIRS, 2, 4, 16, 256), BF16),
        pltpu.VMEM((PAIRS, 2, 3, 16, 256), BF16),
        pltpu.VMEM((2, 2, 4, 4, 16, 256), BF16),
        pltpu.VMEM((PAIRS, 16, LATENT), F32),
        pltpu.VMEM((PAIRS, 16, LATENT), BF16),
        pltpu.VMEM((PAIRS, 16, LATENT), BF16),
        dma((4,)), dma((PAIRS,)), dma((PAIRS,)),
        dma((4 + 2 * CHUNKS,)), dma((4 + 2 * CHUNKS,)), dma((PAIRS,)), dma((PAIRS,)),
        dma((2, PAIRS)), dma((2, PAIRS)), dma((3,)), dma((3,)),
        dma((STEPS, PAIRS)), dma((STEPS, PAIRS)), dma((PAIRS,)), dma((PAIRS,)), dma((2,)), dma((2,)),
    ]
    return pl.pallas_call(
        kernel,
        out_shape=(
            jax.ShapeDtypeStruct((BLOCK, 2048), BF16),
            jax.ShapeDtypeStruct((BLOCK, 1024), BF16),
            jax.ShapeDtypeStruct((BLOCK, LATENT), F32),
            jax.ShapeDtypeStruct((ROPE, BLOCK), F32),
            jax.ShapeDtypeStruct((16, LATENT), F32),
        ),
        in_specs=[hbm] * 7,
        out_specs=(pl.BlockSpec(memory_space=pltpu.VMEM),) * 5,
        scratch_shapes=scratch,
        compiler_params=pltpu.CompilerParams(
            collective_id=0, has_side_effects=True, vmem_limit_bytes=VMEM_BYTES
        ),
        name="latent_attention_grads",
    )(*(pltpu.with_memory_space_constraint(a, pltpu.HBM) for a in arrays))


def write_kernel(count, *refs):
    sources, targets, sems = refs[:count], refs[count:2 * count], refs[2 * count]
    copies = [pltpu.make_async_copy(sources[n], targets[n], sems.at[n]) for n in range(count)]
    for copy in copies:
        copy.start()
    for copy in copies:
        copy.wait()


def write(values):
    count = len(values)
    return pl.pallas_call(
        functools.partial(write_kernel, count),
        out_shape=tuple(jax.ShapeDtypeStruct(value.shape, value.dtype) for value in values),
        in_specs=[pl.BlockSpec(memory_space=pltpu.VMEM)] * count,
        out_specs=(pl.BlockSpec(memory_space=pltpu.HBM),) * count,
        scratch_shapes=[pltpu.SemaphoreType.DMA((count,))],
        name="write_results",
    )(*(pltpu.with_memory_space_constraint(v, pltpu.VMEM) for v in values))


def body(q_nope, q_rope, dout, latent, rope_key, doc_ids, w_up):
    outs = write(fused(
        q_nope[0], q_rope[0], dout[0], latent[0], rope_key[0].T, doc_ids,
        w_up.reshape(2, PAIRS, 2, DIM, LATENT),
    ))
    return (outs[0][None], outs[1][None], outs[2][None], outs[3].T[None], outs[4])


def solution(mesh):
    return jax.shard_map(
        body,
        mesh=mesh,
        in_specs=(
            P("dp", "ctx", None),
            P("dp", "ctx", None),
            P("dp", "ctx", None),
            P("dp", "ctx", None),
            P("dp", "ctx", None),
            P("dp", None),
            P(),
        ),
        out_specs=(
            P("dp", "ctx", None),
            P("dp", "ctx", None),
            P("dp", "ctx", None),
            P("dp", "ctx", None),
            P(("ctx", "dp"), None),
        ),
        check_vma=False,
    )
```

time: 54.2 us -> 40.2 us (0.74)
  the two profiles are of different devices: /device:TPU:224 before, /device:TPU:1 now
where the time goes in v2:
time: 40.2 us; the launch traced here: 40.1 us
  Pallas kernels  39.4 us (98%)
  between operations  0.64 us (2%)
    pallas_call x1, Pallas kernels, fused(): pl.pallas_call(kernel, out_shape=(jax.ShapeDtypeStruct((BLOCK, 2048), BF1...  38.4 us
    pallas_call x1, Pallas kernels, write(): pl.pallas_call(functools.partial(write_kernel, count), out_shape=tuple((j...  1.02 us

profile of v2, /device:TPU:1, one launch (start us, length us, event | category | flops | bytes accessed | tf_op | source)
XLA Modules:
  0.0 40.1 jit_solution(5289444546421932495)
XLA Ops:
  0.6 38.4 %latent_attention_grads.1 = (bf16[128,2048]{1,0:T(8,128)(2,1)S(1)}, bf16[128,1024]{1,0:T(8,128)(2,1)S(1)}, f32[128,512]{1,0:T(8,128)S(1)}, f32[64,128]{1,0:T(8,128)S(1)}, f32[16,512]{1,0:T(8,128)S(1)}) custom-call(bf16[128,2048]{1,0:T(8,128)(2,1)} %bitcast.15, bf16[128,1024]{1,0:T(8,128)(2,1)} %bitcast.17, bf16[128,2048]{1,0:T(8,128)(2,1)} %bitcast.16, ...), custom_call_target="tpu_custom_call" | custom-call | tf_op jit(solution)/shard_map/latent_attention_grads/pallas_call | solution.py:480
  39.1 1.0 %write_results.1 = (bf16[128,2048]{1,0:T(8,128)(2,1)}, bf16[128,1024]{1,0:T(8,128)(2,1)}, f32[128,512]{1,0:T(8,128)}, f32[64,128]{1,0:T(8,128)}, f32[16,512]{1,0:T(8,128)}) custom-call(bf16[128,2048]{1,0:T(8,128)(2,1)S(1)} %get-tuple-element.15.refs_0_, bf16[128,1024]{1,0:T(8,128)(2,1)S(1)} %get-tuple-element.16.refs_1_, ...), custom_call_target="tpu_custom_call" | custom-call | tf_op jit(solution)/shard_map/write_results/pallas_call | solution.py:510

commit v3 on v2

--- a/solution.py
+++ b/solution.py
@@ -235,10 +235,10 @@
         arriving.wait_recv()
         onward.start()
     rope_fwd.wait_recv()
+    spread_rope(0)
+    spread_rope(1)
     for copy in lat_fwd:
         copy.wait_recv()
-    spread_rope(0)
-    spread_rope(1)
 
     def pair_on(offset):
         return lax.rem(z + offset, PAIRS)
@@ -382,12 +382,12 @@
     lax.fori_loop(0, 2, query_grads, 0)
     combine()
     step_two(pair_on(5))
-    finish_plane(3)
     lax.fori_loop(2, 4, query_grads, 0)
     step_two(pair_on(2))
     merge_near()
+    step_two(pair_on(6))
+    finish_plane(3)
     finish_plane(4)
-    step_two(pair_on(6))
     finish_plane(5)
     finish_plane(2)
 

time: 40.2 us -> 37.9 us (0.943)
  Pallas kernels: 39.4 us -> 37.2 us
    pallas_call x1, Pallas kernels: 38.4 us -> 36.1 us  [fused(): pl.pallas_call(kernel, out_shape=(jax.ShapeDtypeStruct((BLOCK, 2048), BF1...]
where the time goes in v3:
time: 37.9 us; the launch traced here: 37.8 us
  Pallas kernels  37.2 us (98%)
  between operations  0.64 us (2%)
    pallas_call x1, Pallas kernels, fused(): pl.pallas_call(kernel, out_shape=(jax.ShapeDtypeStruct((BLOCK, 2048), BF1...  36.1 us
    pallas_call x1, Pallas kernels, write(): pl.pallas_call(functools.partial(write_kernel, count), out_shape=tuple((j...  1.02 us

profile of v3, /device:TPU:1, one launch (start us, length us, event | category | flops | bytes accessed | tf_op | source)
XLA Modules:
  0.0 37.8 jit_solution(7380911207813182122)
XLA Ops:
  0.6 36.1 %latent_attention_grads.1 = (bf16[128,2048]{1,0:T(8,128)(2,1)S(1)}, bf16[128,1024]{1,0:T(8,128)(2,1)S(1)}, f32[128,512]{1,0:T(8,128)S(1)}, f32[64,128]{1,0:T(8,128)S(1)}, f32[16,512]{1,0:T(8,128)S(1)}) custom-call(bf16[128,2048]{1,0:T(8,128)(2,1)} %bitcast.15, bf16[128,1024]{1,0:T(8,128)(2,1)} %bitcast.17, bf16[128,2048]{1,0:T(8,128)(2,1)} %bitcast.16, ...), custom_call_target="tpu_custom_call" | custom-call | tf_op jit(solution)/shard_map/latent_attention_grads/pallas_call | solution.py:480
  36.8 1.0 %write_results.1 = (bf16[128,2048]{1,0:T(8,128)(2,1)}, bf16[128,1024]{1,0:T(8,128)(2,1)}, f32[128,512]{1,0:T(8,128)}, f32[64,128]{1,0:T(8,128)}, f32[16,512]{1,0:T(8,128)}) custom-call(bf16[128,2048]{1,0:T(8,128)(2,1)S(1)} %get-tuple-element.15.refs_0_, bf16[128,1024]{1,0:T(8,128)(2,1)S(1)} %get-tuple-element.16.refs_1_, ...), custom_call_target="tpu_custom_call" | custom-call | tf_op jit(solution)/shard_map/write_results/pallas_call | solution.py:510

commit v4 on v3

--- a/solution.py
+++ b/solution.py
@@ -44,7 +44,7 @@
     q_nope, q_rope, dout, latent, rope_key, docs, w_up,
     qn_out, qr_out, lat_out, rope_out, up_out,
     lat, ropes, rope_tile, doc_row, bias, w, qd, qg, qr_in, gkv, rope_grad, lgf, lgs, lgr,
-    kv_own, scores_own, products_own, grad_scores_kept, k_kept, part, in1, total, out2, in2, near_in, zf, zb, zin,
+    kv_own, scores_own, products_own, own_rows_of, grad_scores_kept, k_kept, part, in1, total, out2, in2, near_in, zf, zb, zin,
     local_sem, head_sem, w_sem,
     lat_send, lat_recv, q_send, q_recv, g_send, g_recv, lg_send, lg_recv,
     rs_send, rs_recv, z_send, z_recv, near_send, near_recv,
@@ -224,8 +224,14 @@
         products = [nt(kv[:, n * 256 + DIM:(n + 1) * 256], qd[j, :, 256:]) for n, j in enumerate(heads)]
         for n, j in enumerate(heads):
             k_kept[j, 256:] = keys[n]
-            scores_own[j] = scores[n] * (SCALE * LOG2E) + bias[256:]
+            score = scores[n] * (SCALE * LOG2E) + bias[256:]
+            highest = jnp.max(score, axis=0, keepdims=True)
+            weights = jnp.exp2(score - highest)
+            scores_own[j] = weights
             products_own[j] = products[n]
+            own_rows_of[j, 0:1] = highest
+            own_rows_of[j, 1:2] = jnp.sum(weights, axis=0, keepdims=True)
+            own_rows_of[j, 2:3] = jnp.sum(weights * products[n], axis=0, keepdims=True)
         return 0
 
     lax.fori_loop(0, PAIRS // 2, own_keys, 0)
@@ -243,11 +249,14 @@
     def pair_on(offset):
         return lax.rem(z + offset, PAIRS)
 
+    def send_part(j, half, index, step, on):
+        remote(part.at[j, half, index], in1.at[j, half, step - 1],
+               rs_send.at[0, j], rs_recv.at[0, j], on(step)).start()
+
     def send_first(j):
         for half, (index, on) in enumerate(first):
             for step in range(1, 4):
-                remote(part.at[j, half, lax.rem(index + step, 4)], in1.at[j, half, step - 1],
-                       rs_send.at[0, j], rs_recv.at[0, j], on(step)).start()
+                send_part(j, half, lax.rem(index + step, 4), step, on)
 
     def attend(i, _):
         heads = [pair_on(offset) for offset in offsets(i)]
@@ -259,11 +268,17 @@
         probs_low, grad_scores = [], []
         for n, j in enumerate(heads):
             k_kept[j, :256] = keys[n]
-            score = jnp.concatenate([scores[n] * (SCALE * LOG2E) + bias[:256], scores_own[j]], axis=0)
+            score = scores[n] * (SCALE * LOG2E) + bias[:256]
+            own_highest = own_rows_of[j, 0:1]
+            highest = jnp.maximum(jnp.max(score, axis=0, keepdims=True), own_highest)
+            weights = jnp.exp2(score - highest)
+            factor = jnp.exp2(own_highest - highest)
+            inverse = 1.0 / (jnp.sum(weights, axis=0, keepdims=True) + own_rows_of[j, 1:2] * factor)
+            probs = jnp.concatenate([weights * inverse, scores_own[j] * (factor * inverse)], axis=0)
+            delta = (
+                jnp.sum(weights * products[n], axis=0, keepdims=True) + own_rows_of[j, 2:3] * factor
+            ) * inverse
             grad_probs = jnp.concatenate([products[n], products_own[j]], axis=0)
-            weights = jnp.exp2(score - jnp.max(score, axis=0, keepdims=True))
-            probs = weights * (1.0 / jnp.sum(weights, axis=0, keepdims=True))
-            delta = jnp.sum(probs * grad_probs, axis=0, keepdims=True)
             probs_low.append(probs.astype(BF16))
             grad_scores.append((probs * ((grad_probs - delta) * SCALE)).astype(BF16))
         rope_sum = rope_grad[...]
@@ -297,16 +312,15 @@
         for n, device in enumerate((above, below)):
             remote(near_in.at[n], near_in.at[n], near_send.at[n], near_recv.at[n], device).wait_recv()
 
-        def merge_part(index, _):
-            for half in range(2):
+        for step in (2, 1, 3, 0):
+            for half, (own, on) in enumerate(first):
+                index = lax.rem(own + step, 4)
                 part[z, half, index] = (
                     part[z, half, index].astype(F32)
                     + near_in[0, half, index].astype(F32) + near_in[1, half, index].astype(F32)
                 ).astype(BF16)
-            return 0
-
-        lax.fori_loop(0, 4, merge_part, 0)
-        send_first(z)
+                if step:
+                    send_part(z, half, index, step, on)
 
     def query_grads(i, _):
         heads = (2 * i, 2 * i + 1)
@@ -391,6 +405,9 @@
     finish_plane(5)
     finish_plane(2)
 
+    step_two(z)
+    finish_plane(6)
+
     def finish_head(j, _):
         head = 2 * j + other
         remote(qg.at[j, sib_rows, pl.ds(0, DIM)], qn_out.at[:, columns(head)],
@@ -412,8 +429,6 @@
     for copy in (rope_next, *lat_next, lat_sib, rope_sib, *lat_fwd, rope_fwd, lg_block, lg_own, lg_back):
         copy.wait_send()
 
-    step_two(z)
-    finish_plane(6)
     step_three(z)
     up_out[...] = zf[z]
 
@@ -461,6 +476,7 @@
         pltpu.VMEM((256, PAIRS * 256), BF16),
         pltpu.VMEM((PAIRS, 256, 256), F32),
         pltpu.VMEM((PAIRS, 256, 256), F32),
+        pltpu.VMEM((PAIRS, 8, 256), F32),
         pltpu.VMEM((PAIRS, 512, 256), BF16),
         pltpu.VMEM((PAIRS, 512, 256), BF16),
         pltpu.VMEM((PAIRS, 2, 4, 4, 16, 256), BF16),

time: 37.9 us -> 37.4 us (0.987)
  Pallas kernels: 37.2 us -> 36.7 us
    pallas_call x1, Pallas kernels: 36.1 us -> 35.6 us  [fused(): pl.pallas_call(kernel, out_shape=(jax.ShapeDtypeStruct((BLOCK, 2048), BF1...]
where the time goes in v4:
time: 37.4 us; the launch traced here: 37.3 us
  Pallas kernels  36.7 us (98%)
  between operations  0.64 us (2%)
    pallas_call x1, Pallas kernels, fused(): pl.pallas_call(kernel, out_shape=(jax.ShapeDtypeStruct((BLOCK, 2048), BF1...  35.6 us
    pallas_call x1, Pallas kernels, write(): pl.pallas_call(functools.partial(write_kernel, count), out_shape=tuple((j...  1.02 us

profile of v4, /device:TPU:1, one launch (start us, length us, event | category | flops | bytes accessed | tf_op | source)
XLA Modules:
  0.0 37.3 jit_solution(11482999859828593487)
XLA Ops:
  0.6 35.6 %latent_attention_grads.1 = (bf16[128,2048]{1,0:T(8,128)(2,1)S(1)}, bf16[128,1024]{1,0:T(8,128)(2,1)S(1)}, f32[128,512]{1,0:T(8,128)S(1)}, f32[64,128]{1,0:T(8,128)S(1)}, f32[16,512]{1,0:T(8,128)S(1)}) custom-call(bf16[128,2048]{1,0:T(8,128)(2,1)} %bitcast.15, bf16[128,1024]{1,0:T(8,128)(2,1)} %bitcast.17, bf16[128,2048]{1,0:T(8,128)(2,1)} %bitcast.16, ...), custom_call_target="tpu_custom_call" | custom-call | tf_op jit(solution)/shard_map/latent_attention_grads/pallas_call | solution.py:496
  36.3 1.0 %write_results.1 = (bf16[128,2048]{1,0:T(8,128)(2,1)}, bf16[128,1024]{1,0:T(8,128)(2,1)}, f32[128,512]{1,0:T(8,128)}, f32[64,128]{1,0:T(8,128)}, f32[16,512]{1,0:T(8,128)}) custom-call(bf16[128,2048]{1,0:T(8,128)(2,1)S(1)} %get-tuple-element.15.refs_0_, bf16[128,1024]{1,0:T(8,128)(2,1)S(1)} %get-tuple-element.16.refs_1_, ...), custom_call_target="tpu_custom_call" | custom-call | tf_op jit(solution)/shard_map/write_results/pallas_call | solution.py:526

commit v5 on v4

--- a/solution.py
+++ b/solution.py
@@ -44,7 +44,7 @@
     q_nope, q_rope, dout, latent, rope_key, docs, w_up,
     qn_out, qr_out, lat_out, rope_out, up_out,
     lat, ropes, rope_tile, doc_row, bias, w, qd, qg, qr_in, gkv, rope_grad, lgf, lgs, lgr,
-    kv_own, scores_own, products_own, own_rows_of, grad_scores_kept, k_kept, part, in1, total, out2, in2, near_in, zf, zb, zin,
+    kv_own, kv_held, scores_own, products_own, own_rows_of, grad_scores_kept, k_kept, part, in1, total, out2, in2, near_in, zf, zb, zin,
     local_sem, head_sem, w_sem,
     lat_send, lat_recv, q_send, q_recv, g_send, g_recv, lg_send, lg_recv,
     rs_send, rs_recv, z_send, z_recv, near_send, near_recv,
@@ -258,13 +258,19 @@
             for step in range(1, 4):
                 send_part(j, half, lax.rem(index + step, 4), step, on)
 
+    def expand(turn):
+        for n, offset in enumerate(offsets(turn)):
+            rows = pl.ds(pl.multiple_of(pair_on(offset) * 256, 256), 256)
+            kv_held[n] = nt(lat[:256], w[rows]).astype(BF16)
+
     def attend(i, _):
         heads = [pair_on(offset) for offset in offsets(i)]
-        kv = [nt(lat[:256], w[pl.ds(pl.multiple_of(j * 256, 256), 256)]).astype(BF16) for j in heads]
+        kv = [kv_held[n] for n in range(2)]
         rope = rope_tile[:256]
         keys = [jnp.concatenate([kv[n][:, :DIM], rope], axis=1) for n in range(2)]
         scores = [nt(keys[n], qd[j, :, :256]) for n, j in enumerate(heads)]
         products = [nt(kv[n][:, DIM:], qd[j, :, 256:]) for n, j in enumerate(heads)]
+        expand(lax.rem(i + 1, PAIRS // 2))
         probs_low, grad_scores = [], []
         for n, j in enumerate(heads):
             k_kept[j, :256] = keys[n]
@@ -389,6 +395,7 @@
         step_three(pair_on(offset))
         step_four(pair_on(offset))
 
+    expand(0)
     lax.fori_loop(0, PAIRS // 2, attend, 0)
     step_two(pair_on(3))
     project()
@@ -474,6 +481,7 @@
         pltpu.VMEM((3, BLOCK, LATENT + DIM), BF16),
         pltpu.VMEM((3, BLOCK, LATENT + DIM), BF16),
         pltpu.VMEM((256, PAIRS * 256), BF16),
+        pltpu.VMEM((2, 256, 256), BF16),
         pltpu.VMEM((PAIRS, 256, 256), F32),
         pltpu.VMEM((PAIRS, 256, 256), F32),
         pltpu.VMEM((PAIRS, 8, 256), F32),

time: 37.4 us -> 37.3 us (level)
  no operation moved by 1% of the time
where the time goes in v5:
time: 37.3 us; the launch traced here: 37.2 us
  Pallas kernels  36.6 us (98%)
  between operations  0.64 us (2%)
    pallas_call x1, Pallas kernels, fused(): pl.pallas_call(kernel, out_shape=(jax.ShapeDtypeStruct((BLOCK, 2048), BF1...  35.6 us
    pallas_call x1, Pallas kernels, write(): pl.pallas_call(functools.partial(write_kernel, count), out_shape=tuple((j...  1.02 us

profile of v5, /device:TPU:1, one launch (start us, length us, event | category | flops | bytes accessed | tf_op | source)
XLA Modules:
  0.0 37.2 jit_solution(5730310107466121002)
XLA Ops:
  0.6 35.6 %latent_attention_grads.1 = (bf16[128,2048]{1,0:T(8,128)(2,1)S(1)}, bf16[128,1024]{1,0:T(8,128)(2,1)S(1)}, f32[128,512]{1,0:T(8,128)S(1)}, f32[64,128]{1,0:T(8,128)S(1)}, f32[16,512]{1,0:T(8,128)S(1)}) custom-call(bf16[128,2048]{1,0:T(8,128)(2,1)} %bitcast.15, bf16[128,1024]{1,0:T(8,128)(2,1)} %bitcast.17, bf16[128,2048]{1,0:T(8,128)(2,1)} %bitcast.16, ...), custom_call_target="tpu_custom_call" | custom-call | tf_op jit(solution)/shard_map/latent_attention_grads/pallas_call | solution.py:504
  36.2 1.0 %write_results.1 = (bf16[128,2048]{1,0:T(8,128)(2,1)}, bf16[128,1024]{1,0:T(8,128)(2,1)}, f32[128,512]{1,0:T(8,128)}, f32[64,128]{1,0:T(8,128)}, f32[16,512]{1,0:T(8,128)}) custom-call(bf16[128,2048]{1,0:T(8,128)(2,1)S(1)} %get-tuple-element.15.refs_0_, bf16[128,1024]{1,0:T(8,128)(2,1)S(1)} %get-tuple-element.16.refs_1_, ...), custom_call_target="tpu_custom_call" | custom-call | tf_op jit(solution)/shard_map/write_results/pallas_call | solution.py:534
